TPU v7x, 32 devices: a whole 2x2x4 slice. The times are simulated.
32 devices in a mesh: node: 8 (over z, x), freq: 4 (over y, core).
Axes of the slice: x: 2, y: 2, z: 4, core: 2. Of those that a mesh axis runs over, the one named last changes fastest.
Arguments:
- receiver_gathers: float32 [256, 393216], P('node', 'freq'), may hold values from -6 to 6
- fourier_estimate: float32 [64, 2, 256, 384], P(('node', 'freq')), may hold values from -6 to 6
- random_projector: float32 [384, 48], replicated, may hold values from -0.3125 to 0.3125
- release_sample: int32 [384], P('freq'), may hold values from 0 to 393215, as said below
Outputs:
- deblended: float32 [64, 2, 256, 384], P(('node', 'freq'))
- misfit_signal: float32 [256, 393216], P('node', 'freq')
Inputs may be any that keep to these rules, and one draw needn't show every extreme that they name: `release_sample`: shot s fires at a sample of [s * 1024, (s + 1) * 1024).
All inputs are finite; a program needn't handle non-finite values.
Results may differ from a plain program's by a relative error of at most 0.0003.
Values sent between devices are 32-bit elements; how exact they have to be, the bound alone decides.
A program may use at most 192 MiB of HBM per device.

v0:
```python
import math

import jax
import jax.numpy as jnp
from jax import lax
from jax.sharding import PartitionSpec as P

LISTEN_SPAN = 4096
SOURCE_SPACING = 1024


relaxation = 0.25
ridge_scale = 0.001
highest = lax.Precision.HIGHEST


def from_behind(array, axis, by):
    size = lax.axis_size(axis)
    pairs = [(i, i + by) for i in range(size) if 0 <= i + by < size]
    return lax.ppermute(array, axis, pairs)


def dft_table(bin_count, length):
    spectral_columns = lax.iota(jnp.int32, bin_count) + 1
    sample_times = lax.iota(jnp.int32, length)
    phases = spectral_columns[:, None] * sample_times[None, :] % LISTEN_SPAN
    phase_angles = 2.0 * math.pi / LISTEN_SPAN * phases.astype(jnp.float32)
    inverse_root = 1.0 / math.sqrt(LISTEN_SPAN)
    return jnp.stack(
        [jnp.cos(phase_angles) * inverse_root, -jnp.sin(phase_angles) * inverse_root], axis=1
    )


def inner_product(former, latter):
    return lax.dot_general(former, latter, (((1,), (1,)), ((), ())), precision=highest)


def outer_product(former, latter):
    return lax.dot_general(former, latter, (((0,), (0,)), ((), ())), precision=highest)


def reduce_rank(matrix, random_projector):
    real_part = matrix[0]
    imag_part = matrix[1]
    rank_count = random_projector.shape[1]
    proj_real = lax.dot_general(
        random_projector, real_part, (((0,), (1,)), ((), ())), precision=highest
    )
    proj_imag = lax.dot_general(
        random_projector, imag_part, (((0,), (1,)), ((), ())), precision=highest
    )
    gram_real = inner_product(proj_real, proj_real) + inner_product(proj_imag, proj_imag)
    gram_imag = inner_product(proj_real, proj_imag) - inner_product(proj_imag, proj_real)
    coef_real = jnp.dot(proj_real, real_part, precision=highest) + jnp.dot(
        proj_imag, imag_part, precision=highest
    )
    coef_imag = jnp.dot(proj_real, imag_part, precision=highest) - jnp.dot(
        proj_imag, real_part, precision=highest
    )
    system = jnp.concatenate(
        [jnp.concatenate([gram_real, -gram_imag], 1), jnp.concatenate([gram_imag, gram_real], 1)], 0
    )
    ridge_shift = ridge_scale * jnp.trace(gram_real) / rank_count
    system = system + ridge_shift * jnp.eye(2 * rank_count, dtype=system.dtype)
    factor = jnp.linalg.cholesky(system)
    right_side = jnp.concatenate([coef_real, coef_imag], 0)
    halfway = lax.linalg.triangular_solve(factor, right_side, left_side=True, lower=True)
    solved = lax.linalg.triangular_solve(
        factor, halfway, left_side=True, lower=True, transpose_a=True
    )
    solution_real = solved[:rank_count]
    solution_imag = solved[rank_count:]
    low_real = outer_product(proj_real, solution_real) - outer_product(proj_imag, solution_imag)
    low_imag = outer_product(proj_real, solution_imag) + outer_product(proj_imag, solution_real)
    return jnp.stack([low_real, low_imag])


def shards(receiver_gathers, fourier_estimate, random_projector, release_sample):
    receiver_portion, segment = receiver_gathers.shape
    freq_local = fourier_estimate.shape[0]
    source_position = release_sample.shape[0]
    node_axis = lax.axis_size("node")
    freq_axis = lax.axis_size("freq")
    freq_total = freq_local * node_axis * freq_axis
    listen_segments = LISTEN_SPAN // SOURCE_SPACING + 1
    segment_extent = listen_segments * SOURCE_SPACING
    dft_rows = dft_table(freq_total, segment_extent).reshape(2 * freq_total, segment_extent)
    random_dither = release_sample % SOURCE_SPACING
    spectral_columns = lax.iota(jnp.int32, freq_total) + 1
    delay_rotation = spectral_columns[:, None] * random_dither[None, :] % LISTEN_SPAN
    shift_angle = 2.0 * math.pi / LISTEN_SPAN * delay_rotation.astype(jnp.float32)
    cos_shift = jnp.cos(shift_angle)[:, None, :]
    sin_shift = jnp.sin(shift_angle)[:, None, :]
    segment_clock = lax.iota(jnp.int32, segment_extent)
    within_mask = (segment_clock[None, :] >= random_dither[:, None]) & (
        segment_clock[None, :] < random_dither[:, None] + LISTEN_SPAN
    )
    window_mask = within_mask.astype(jnp.float32)
    regrouped_traces = fourier_estimate.reshape(
        freq_local, 2, node_axis, receiver_portion, freq_axis, source_position
    )
    regrouped_traces = jnp.transpose(regrouped_traces, (2, 4, 0, 1, 3, 5)).reshape(
        node_axis * freq_axis, freq_local, 2, receiver_portion, source_position
    )
    gathered = lax.all_to_all(
        regrouped_traces, ("node", "freq"), split_axis=0, concat_axis=1, tiled=True
    )
    gathered = gathered.reshape(freq_total, 2, receiver_portion, source_position)
    real_in = gathered[:, 0]
    imag_in = gathered[:, 1]
    shifted_real = real_in * cos_shift + imag_in * sin_shift
    shifted_imag = imag_in * cos_shift - real_in * sin_shift
    coeffs = jnp.stack([shifted_real, shifted_imag], axis=1).reshape(
        2 * freq_total, receiver_portion * source_position
    )
    accumulated_total = jnp.zeros(
        (receiver_portion, source_position + listen_segments - 1, SOURCE_SPACING), jnp.float32
    )
    for offset in range(listen_segments):
        table_block = dft_rows[:, offset * SOURCE_SPACING : (offset + 1) * SOURCE_SPACING]
        mask_block = window_mask[:, offset * SOURCE_SPACING : (offset + 1) * SOURCE_SPACING]
        frame_block = 2.0 * lax.dot_general(
            coeffs, table_block, (((0,), (0,)), ((), ())), precision=highest
        )
        frame_block = (
            frame_block.reshape(receiver_portion, source_position, SOURCE_SPACING)
            * mask_block[None]
        )
        accumulated_total = accumulated_total + jnp.pad(
            frame_block, ((0, 0), (offset, listen_segments - 1 - offset), (0, 0))
        )
    merged = accumulated_total.reshape(receiver_portion, segment + LISTEN_SPAN)
    carried = from_behind(merged[:, segment:], "freq", 1)
    mixed_signal = jnp.concatenate(
        [merged[:, :LISTEN_SPAN] + carried, merged[:, LISTEN_SPAN:segment]], 1
    )
    misfit_signal = receiver_gathers - mixed_signal
    heads = from_behind(misfit_signal[:, :LISTEN_SPAN], "freq", -1)
    extended = jnp.concatenate([misfit_signal, heads], 1).reshape(
        receiver_portion, source_position + listen_segments - 1, SOURCE_SPACING
    )
    transformed = jnp.zeros((2 * freq_total, receiver_portion * source_position), jnp.float32)
    for offset in range(listen_segments):
        table_block = dft_rows[:, offset * SOURCE_SPACING : (offset + 1) * SOURCE_SPACING]
        mask_block = window_mask[:, offset * SOURCE_SPACING : (offset + 1) * SOURCE_SPACING]
        piece_block = (extended[:, offset : offset + source_position] * mask_block[None]).reshape(
            receiver_portion * source_position, SOURCE_SPACING
        )
        transformed = transformed + lax.dot_general(
            table_block, piece_block, (((1,), (1,)), ((), ())), precision=highest
        )
    transformed = transformed.reshape(freq_total, 2, receiver_portion, source_position)
    cosine_part = transformed[:, 0]
    sine_part = transformed[:, 1]
    adjoint_real = cosine_part * cos_shift - sine_part * sin_shift
    adjoint_imag = sine_part * cos_shift + cosine_part * sin_shift
    adjoint_operator = jnp.stack([adjoint_real, adjoint_imag], axis=1)
    arrived = lax.all_to_all(
        adjoint_operator.reshape(1, freq_total, 2, receiver_portion, source_position),
        ("node", "freq"),
        split_axis=1,
        concat_axis=0,
        tiled=True,
    )
    arrived = arrived.reshape(
        node_axis, freq_axis, freq_local, 2, receiver_portion, source_position
    )
    arrived = jnp.transpose(arrived, (2, 3, 0, 4, 1, 5)).reshape(
        freq_local, 2, node_axis * receiver_portion, freq_axis * source_position
    )
    updated = fourier_estimate + relaxation * arrived
    deblended = jax.vmap(reduce_rank, in_axes=(0, None))(updated, random_projector)
    return (deblended, misfit_signal)


def solution(mesh):
    return jax.shard_map(
        shards,
        mesh=mesh,
        in_specs=(P("node", "freq"), P(("node", "freq"), None, None, None), P(), P("freq")),
        out_specs=(P(("node", "freq"), None, None, None), P("node", "freq")),
        check_vma=False,
    )
```

profile of v0, /device:TPU:0, one launch (start us, length us, event | category | flops | bytes accessed | tf_op | source)
XLA Modules:
  0.0 497.0 jit_solution(12386130168117259652)
XLA Ops:
  0.6 2.6 reshape.271
  4.8 7.4 %all-to-all-start = ((f32[32,2,2,32,96]{4,3,2,1,0:T(8,128)}), f32[32,2,2,32,96]{4,3,2,1,0:T(8,128)}, u32[]{:S(2)}, u32[]{:S(2)}) async-start(f32[32,2,2,32,96]{4,3,2,1,0:T(8,128)} %bitcast.112), calls=%async_computation | async-start | bytes 4194304 | tf_op jit(solution)/shard_map/all_to_all | solution.py:105
  12.3 5.2 %cosine_multiply_fusion = (f32[64,1,5120]{2,0,1:T(8,128)S(1)}, f32[64,1,5120]{2,0,1:T(8,128)S(1)}) fusion(s32[64]{0:T(128)S(1)} %iota_add_fusion), kind=kLoop, calls=%fused_computation.39 | loop fusion | flops 5570560 | bytes 2621696 | tf_op jit(solution)/shard_map/mul | solution.py:30
  19.8 2.9 reshape.270
  24.3 36.8 %all-to-all-done = f32[32,2,2,32,96]{4,3,2,1,0:T(8,128)} async-done(((f32[32,2,2,32,96]{4,3,2,1,0:T(8,128)}), f32[32,2,2,32,96]{4,3,2,1,0:T(8,128)}, u32[]{:S(2)}, u32[]{:S(2)}) %all-to-all-start) | async-done | bytes 1572896 | tf_op jit(solution)/shard_map/all_to_all | solution.py:105
  64.5 2.5 reshape.274
  67.0 14.7 %convolution_multiply_fusion.3 = f32[3072,1024]{1,0:T(8,128)} fusion(f32[128,3072]{1,0:T(8,128)S(1)} %reshape.274, f32[128,5120]{1,0:T(8,128)} %reshape.270), kind=kOutput, calls=%fused_computation.11 | convolution fusion | flops 4834983936 | bytes 14680064 | tf_op jit(solution)/shard_map/dot_general | solution.py:122
  81.7 12.6 %convolution_multiply_fusion.2 = f32[3072,1024]{1,0:T(8,128)} fusion(f32[128,3072]{1,0:T(8,128)S(1)} %reshape.274, f32[128,5120]{1,0:T(8,128)S(1)} %copy-done.3), kind=kOutput, calls=%fused_computation.10 | convolution fusion | flops 4834983936 | bytes 14680064 | tf_op jit(solution)/shard_map/dot_general | solution.py:122
  94.3 12.5 %convolution_multiply_fusion.1 = f32[3072,1024]{1,0:T(8,128)} fusion(f32[128,3072]{1,0:T(8,128)S(1)} %reshape.274, f32[128,5120]{1,0:T(8,128)S(1)} %copy-done.3), kind=kOutput, calls=%fused_computation.9 | convolution fusion | flops 4834983936 | bytes 14680064 | tf_op jit(solution)/shard_map/dot_general | solution.py:122
  106.8 13.0 %convolution_multiply_fusion = f32[3072,1024]{1,0:T(8,128)} fusion(f32[128,3072]{1,0:T(8,128)S(1)} %reshape.274, f32[128,5120]{1,0:T(8,128)S(1)} %copy-done.3), kind=kOutput, calls=%fused_computation.8 | convolution fusion | flops 4834983936 | bytes 14680064 | tf_op jit(solution)/shard_map/dot_general | solution.py:122
  119.8 12.5 %convolution_multiply_fusion.4 = f32[3072,1024]{1,0:T(8,128)} fusion(f32[128,3072]{1,0:T(8,128)S(1)} %reshape.274, f32[128,5120]{1,0:T(8,128)S(1)} %copy-done.3), kind=kOutput, calls=%fused_computation.12 | convolution fusion | flops 4834983936 | bytes 14680064 | tf_op jit(solution)/shard_map/dot_general | solution.py:122
  132.3 12.1 %broadcast_multiply_fusion.4 = f32[32,96,1024]{2,1,0:T(8,128)} fusion(f32[32,96,1024]{2,1,0:T(8,128)} %bitcast.105, f32[96,1024]{1,0:T(8,128)S(1)} %copy-done.5), kind=kLoop, calls=%fused_computation.17 | loop fusion | flops 3145728 | bytes 25559040 | tf_op jit(solution)/shard_map/mul | solution.py:126
  144.4 19.8 %broadcast_multiply_fusion.2 = (f32[32,96,1024]{2,1,0:T(8,128)}, f32[32,96,1024]{2,1,0:T(8,128)}) fusion(f32[32,96,1024]{2,1,0:T(8,128)} %bitcast.109, f32[96,1024]{1,0:T(8,128)S(1)} %get-tuple-element.30, f32[32,96,1024]{2,1,0:T(8,128)} %bitcast.108, f32[96,1024]{1,0:T(8,128)S(1)} %get-tuple-element.31), kind=kLoop, calls=%fused_computation.15 | loop fusion | flops 6291456 | bytes 51118080 | tf_op jit(solution)/shard_map/mul | solution.py:126
  164.2 20.9 %broadcast_multiply_fusion = (f32[32,96,1024]{2,1,0:T(8,128)}, f32[32,96,1024]{2,1,0:T(8,128)}) fusion(f32[32,96,1024]{2,1,0:T(8,128)} %bitcast.107, f32[96,1024]{1,0:T(8,128)S(1)} %get-tuple-element.28, f32[32,96,1024]{2,1,0:T(8,128)} %bitcast.106, f32[96,1024]{1,0:T(8,128)S(1)} %get-tuple-element.29), kind=kLoop, calls=%fused_computation.13 | loop fusion | flops 6291456 | bytes 51118080 | tf_op jit(solution)/shard_map/mul | solution.py:126
  185.1 23.0 %pad_add_fusion = f32[32,100,1024]{2,1,0:T(8,128)} fusion(f32[32,96,1024]{2,1,0:T(8,128)} %get-tuple-element.40, f32[32,96,1024]{2,1,0:T(8,128)} %get-tuple-element.41, f32[32,96,1024]{2,1,0:T(8,128)} %get-tuple-element.42, f32[32,96,1024]{2,1,0:T(8,128)} %get-tuple-element.43, f32[32,96,1024]{2,1,0:T(8,128)S(1)} %bitcast.95), kind=kLoop, calls=%fused_computation | loop fusion | flops 13107200 | bytes 76021760 | tf_op jit(solution)/shard_map/add | solution.py:129
  208.1 17.2 %copy.85 = f32[4,8,100,1024]{3,1,2,0:T(8,128)} copy(f32[4,8,100,1024]{3,2,1,0:T(8,128)} %bitcast.90) | data formatting | bytes 26214400
  228.0 9.8 %slice.146 = f32[32,94208]{1,0:T(8,128)} slice(f32[32,102400]{1,0:T(8,128)} %bitcast.92), slice={[0:32], [4096:98304]} | slice | bytes 24117248 | tf_op jit(solution)/shard_map/slice | solution.py:135
  238.9 8.8 %maximum_subtract_fusion = f32[32,98304]{1,0:T(8,128)S(1)} fusion(f32[32,98304]{1,0:T(8,128)} %param.4, f32[32,94208]{1,0:T(8,128)} %slice.146, f32[32,4096]{1,0:T(8,128)S(1)} %slice_add_fusion), kind=kLoop, calls=%fused_computation.7 | loop fusion | flops 6291456 | bytes 37748736 | tf_op jit(solution)/shard_map/sub | solution.py:137
  249.1 3.9 collective-permute-done.1
  253.0 5.6 %pad_maximum_fusion = f32[32,102400]{1,0:T(8,128)} fusion(f32[32,4096]{1,0:T(8,128)S(1)} %collective-permute-done.1, f32[32,98304]{1,0:T(8,128)S(1)} %maximum_subtract_fusion), kind=kLoop, calls=%fused_computation.1 | loop fusion | flops 3276800 | bytes 26214400 | tf_op jit(solution)/shard_map/concatenate | solution.py:139
  258.6 10.4 %reshape.281 = f32[32,100,1024]{2,1,0:T(8,128)} reshape(f32[32,102400]{1,0:T(8,128)} %pad_maximum_fusion) | data formatting | bytes 26214400 | tf_op jit(solution)/shard_map/reshape | solution.py:139
  269.0 42.0 %slice_multiply_fusion = (f32[32,96,1024]{2,1,0:T(8,128)}, f32[32,96,1024]{2,1,0:T(8,128)}, f32[32,96,1024]{2,1,0:T(8,128)}, f32[32,96,1024]{2,1,0:T(8,128)}, f32[32,96,1024]{2,1,0:T(8,128)}) fusion(f32[32,100,1024]{2,1,0:T(8,128)} %reshape.281, f32[96,1024]{1,0:T(8,128)S(1)} %get-tuple-element.28, f32[96,1024]{1,0:T(8,128)S(1)} %get-tuple-element.29, ...), kind=kLoop, calls=%fused_computation.2 | loop fusion | flops 15728640 | bytes 127795200 | tf_op jit(solution)/shard_map/mul | solution.py:146
  311.1 16.3 %fusion.18 = f32[128,3072]{1,0:T(8,128)S(1)} fusion(f32[3072,1024]{1,0:T(8,128)} %bitcast.96, f32[128,5120]{1,0:T(8,128)S(1)} %copy-done.4), kind=kOutput, calls=%fused_computation.69 | convolution fusion | flops 4831838208 | bytes 14680064 | tf_op jit(solution)/shard_map/dot_general | solution.py:149
  327.4 12.9 %convolution_add_fusion.3 = f32[128,3072]{1,0:T(8,128)S(1)} fusion(f32[128,3072]{1,0:T(8,128)S(1)} %fusion.18, f32[3072,1024]{1,0:T(8,128)S(1)} %bitcast.104, f32[128,5120]{1,0:T(8,128)S(1)} %copy-done.4), kind=kOutput, calls=%fused_computation.21 | convolution fusion | flops 4832231424 | bytes 16252928 | tf_op jit(solution)/shard_map/dot_general | solution.py:149
  340.3 16.1 %convolution_add_fusion.2 = f32[128,3072]{1,0:T(8,128)S(1)} fusion(f32[128,3072]{1,0:T(8,128)S(1)} %convolution_add_fusion.3, f32[3072,1024]{1,0:T(8,128)} %bitcast.103, f32[128,5120]{1,0:T(8,128)S(1)} %copy-done.4), kind=kOutput, calls=%fused_computation.20 | convolution fusion | flops 4832231424 | bytes 16252928 | tf_op jit(solution)/shard_map/dot_general | solution.py:149
  356.5 12.9 %convolution_add_fusion.1 = f32[128,3072]{1,0:T(8,128)S(1)} fusion(f32[128,3072]{1,0:T(8,128)S(1)} %convolution_add_fusion.2, f32[3072,1024]{1,0:T(8,128)S(1)} %bitcast.102, f32[128,5120]{1,0:T(8,128)S(1)} %copy-done.4), kind=kOutput, calls=%fused_computation.19 | convolution fusion | flops 4832231424 | bytes 16252928 | tf_op jit(solution)/shard_map/dot_general | solution.py:149
  369.4 14.3 %convolution_add_fusion = f32[128,3072]{1,0:T(8,128)} fusion(f32[128,3072]{1,0:T(8,128)S(1)} %convolution_add_fusion.1, f32[3072,1024]{1,0:T(8,128)S(1)} %bitcast.99, f32[128,5120]{1,0:T(8,128)S(1)} %copy-done.4), kind=kOutput, calls=%fused_computation.18 | convolution fusion | flops 4832231424 | bytes 16252928 | tf_op jit(solution)/shard_map/dot_general | solution.py:149
  387.7 10.5 %all-to-all-start.1 = ((f32[1,64,2,32,96]{4,3,2,0,1:T(8,128)}), f32[1,64,2,32,96]{4,3,2,0,1:T(8,128)S(1)}, u32[]{:S(2)}, u32[]{:S(2)}) async-start(f32[1,64,2,32,96]{4,3,2,0,1:T(8,128)} %maximum_bitcast_fusion), calls=%async_computation.1 | async-start | bytes 4194304 | tf_op jit(solution)/shard_map/all_to_all | solution.py:158
  398.3 48.6 %all-to-all-done.1 = f32[1,64,2,32,96]{4,3,2,0,1:T(8,128)S(1)} async-done(((f32[1,64,2,32,96]{4,3,2,0,1:T(8,128)}), f32[1,64,2,32,96]{4,3,2,0,1:T(8,128)S(1)}, u32[]{:S(2)}, u32[]{:S(2)}) %all-to-all-start.1) | async-done | bytes 1572896 | tf_op jit(solution)/shard_map/all_to_all | solution.py:158
  449.0 2.2 mul.323
  457.3 17.6 %custom-call.9 = f32[2,96,96]{2,1,0:T(8,128)S(1)} custom-call(f32[2,96,96]{2,1,0:T(8,128)S(1)} %fusion.36), custom_call_target="Cholesky" | custom-call | tf_op jit(solution)/shard_map/vmap(jit(cholesky))/cholesky | solution.py:65
  475.2 14.9 %custom-call.10 = f32[2,1,96,96]{2,3,1,0:T(8,128)S(1)} custom-call(f32[2,1,96,96]{3,2,1,0:T(8,128)S(1)} %select_bitcast_fusion), custom_call_target="InvertDiagBlocksLowerTriangular" | custom-call | tf_op jit(solution)/shard_map/vmap()/triangular_solve | solution.py:68
  (97 shorter events, 33.1 us)
Async XLA Ops:
  0.6 452.6 %copy-start = (f32[384,48]{0,1:T(8,128)S(1)}, f32[384,48]{0,1:T(8,128)}, u32[]{:S(2)}) copy-start(f32[384,48]{0,1:T(8,128)} %param.6) | copy-start | bytes 221188
  4.8 56.2 %all-to-all-start = ((f32[32,2,2,32,96]{4,3,2,1,0:T(8,128)}), f32[32,2,2,32,96]{4,3,2,1,0:T(8,128)}, u32[]{:S(2)}, u32[]{:S(2)}) async-start(f32[32,2,2,32,96]{4,3,2,1,0:T(8,128)} %bitcast.112), calls=%async_computation | async-start | bytes 4194304 | tf_op jit(solution)/shard_map/all_to_all | solution.py:105
  19.8 3.0 copy-start.11
  23.0 38.1 %copy-start.7 = (f32[64,96]{1,0:T(8,128)}, f32[64,96]{1,0:T(8,128)S(1)}, u32[]{:S(2)}) copy-start(f32[64,96]{1,0:T(8,128)S(1)} %get-tuple-element.32) | copy-start | bytes 73732
  23.0 38.0 %copy-start.9 = (f32[64,96]{1,0:T(8,128)}, f32[64,96]{1,0:T(8,128)S(1)}, u32[]{:S(2)}) copy-start(f32[64,96]{1,0:T(8,128)S(1)} %get-tuple-element.33) | copy-start | bytes 73732
  67.0 14.7 %copy-start.3 = (f32[128,5120]{1,0:T(8,128)S(1)}, f32[128,5120]{1,0:T(8,128)}, u32[]{:S(2)}) copy-start(f32[128,5120]{1,0:T(8,128)} %reshape.270) | copy-start | bytes 7864324
  119.8 12.5 %copy-start.5 = (f32[96,1024]{1,0:T(8,128)S(1)}, f32[96,1024]{1,0:T(8,128)}, u32[]{:S(2)}) copy-start(f32[96,1024]{1,0:T(8,128)} %get-tuple-element.27) | copy-start | bytes 1179652
  164.2 21.0 %slice-start = ((s8[12582912]{0:T(1024)(128)(4,1)}), s8[4194304]{0:T(1024)(128)(4,1)S(1)}, s32[]{:S(2)}) async-start(s8[12582912]{0:T(1024)(128)(4,1)} %bitcast.94), calls=%async_computation.2 | async-start | bytes 8388608
  164.2 21.0 %slice-start.1 = ((s8[12582912]{0:T(1024)(128)(4,1)}), s8[4194304]{0:T(1024)(128)(4,1)S(1)}, s32[]{:S(2)}) async-start(s8[12582912]{0:T(1024)(128)(4,1)} %bitcast.94), calls=%async_computation.3 | async-start | bytes 8388608
  164.2 21.0 %slice-start.2 = ((s8[12582912]{0:T(1024)(128)(4,1)}), s8[4194304]{0:T(1024)(128)(4,1)S(1)}, s32[]{:S(2)}) async-start(s8[12582912]{0:T(1024)(128)(4,1)} %bitcast.94), calls=%async_computation.4 | async-start | bytes 8388608
  226.4 11.4 %collective-permute-start = (f32[32,4096]{1,0:T(8,128)S(1)}, f32[32,4096]{1,0:T(8,128)S(1)}, u32[]{:S(2)}, u32[]{:S(2)}) collective-permute-start(f32[32,4096]{1,0:T(8,128)S(1)} %slice.145), channel_id=1, source_target_pairs={{0,1},{1,2},{2,3},{4,5},{5,6},{6,7},{8,9},{9,10},{10,11},{12,13},{... | collective-permute-start | bytes 1572872 | tf_op jit(solution)/shard_map/ppermute | solution.py:20
  247.7 5.2 %copy-start.1 = (f32[32,98304]{1,0:T(8,128)}, f32[32,98304]{1,0:T(8,128)S(1)}, u32[]{:S(2)}) copy-start(f32[32,98304]{1,0:T(8,128)S(1)} %maximum_subtract_fusion) | copy-start | bytes 37748740
  247.8 5.2 %collective-permute-start.1 = (f32[32,4096]{1,0:T(8,128)S(1)}, f32[32,4096]{1,0:T(8,128)S(1)}, u32[]{:S(2)}, u32[]{:S(2)}) collective-permute-start(f32[32,4096]{1,0:T(8,128)S(1)} %slice.147), channel_id=1, source_target_pairs={{1,0},{2,1},{3,2},{5,4},{6,5},{7,6},{9,8},{10,9},{11,10},{13,12},{... | collective-permute-start | bytes 1572872 | tf_op jit(solution)/shard_map/ppermute | solution.py:20
  258.6 10.4 %copy-start.6 = (f32[96,1024]{1,0:T(8,128)S(1)}, f32[96,1024]{1,0:T(8,128)}, u32[]{:S(2)}) copy-start(f32[96,1024]{1,0:T(8,128)} %get-tuple-element.27) | copy-start | bytes 1179652
  269.0 42.0 %copy-start.4 = (f32[128,5120]{1,0:T(8,128)S(1)}, f32[128,5120]{1,0:T(8,128)}, u32[]{:S(2)}) copy-start(f32[128,5120]{1,0:T(8,128)} %reshape.270) | copy-start | bytes 7864324
  311.1 16.3 %copy-start.2 = (f32[32,96,1024]{2,1,0:T(8,128)S(1)}, f32[32,96,1024]{2,1,0:T(8,128)}, u32[]{:S(2)}) copy-start(f32[32,96,1024]{2,1,0:T(8,128)} %get-tuple-element.22) | copy-start | bytes 37748740
  327.4 29.0 %slice-start.6 = ((s8[12582912]{0:T(1024)(128)(4,1)}), s8[4194304]{0:T(1024)(128)(4,1)S(1)}, s32[]{:S(2)}) async-start(s8[12582912]{0:T(1024)(128)(4,1)} %bitcast.100), calls=%async_computation.8 | async-start | bytes 8388608
  327.4 29.0 %slice-start.7 = ((s8[12582912]{0:T(1024)(128)(4,1)}), s8[4194304]{0:T(1024)(128)(4,1)S(1)}, s32[]{:S(2)}) async-start(s8[12582912]{0:T(1024)(128)(4,1)} %bitcast.100), calls=%async_computation.9 | async-start | bytes 8388608
  340.3 16.1 %slice-start.8 = ((s8[12582912]{0:T(1024)(128)(4,1)}), s8[4194304]{0:T(1024)(128)(4,1)S(1)}, s32[]{:S(2)}) async-start(s8[12582912]{0:T(1024)(128)(4,1)} %bitcast.100), calls=%async_computation.10 | async-start | bytes 8388608
  340.3 29.1 %slice-start.3 = ((s8[12582912]{0:T(1024)(128)(4,1)}), s8[4194304]{0:T(1024)(128)(4,1)S(1)}, s32[]{:S(2)}) async-start(s8[12582912]{0:T(1024)(128)(4,1)} %bitcast.97), calls=%async_computation.5 | async-start | bytes 8388608
  340.3 29.1 %slice-start.4 = ((s8[12582912]{0:T(1024)(128)(4,1)}), s8[4194304]{0:T(1024)(128)(4,1)S(1)}, s32[]{:S(2)}) async-start(s8[12582912]{0:T(1024)(128)(4,1)} %bitcast.97), calls=%async_computation.6 | async-start | bytes 8388608
  356.5 12.9 %slice-start.5 = ((s8[12582912]{0:T(1024)(128)(4,1)}), s8[4194304]{0:T(1024)(128)(4,1)S(1)}, s32[]{:S(2)}) async-start(s8[12582912]{0:T(1024)(128)(4,1)} %bitcast.97), calls=%async_computation.7 | async-start | bytes 8388608
  383.7 2.1 copy-start.8
  383.7 2.1 copy-start.10
  387.7 59.2 %all-to-all-start.1 = ((f32[1,64,2,32,96]{4,3,2,0,1:T(8,128)}), f32[1,64,2,32,96]{4,3,2,0,1:T(8,128)S(1)}, u32[]{:S(2)}, u32[]{:S(2)}) async-start(f32[1,64,2,32,96]{4,3,2,0,1:T(8,128)} %maximum_bitcast_fusion), calls=%async_computation.1 | async-start | bytes 4194304 | tf_op jit(solution)/shard_map/all_to_all | solution.py:158
where the time goes:
time: 507 us; the launch traced here: 497 us
  other arithmetic  180 us (36%)
  matrix products  147 us (29%)
  waiting for transfers between devices  89.2 us (18%)
  local copies, waits for them, and re-layouts  58.6 us (12%)
  starting transfers between devices  20.8 us (4%)
    dot_general x5, matrix products, shards(): lax.dot_general(table_block, piece_block, (((1,), (1,)), ((), ())), preci...  72.4 us
    dot_general x5, matrix products, shards(): lax.dot_general(coeffs, table_block, (((0,), (0,)), ((), ())), precision=...  65.3 us
    mul x3, other arithmetic, shards(): frame_block.reshape(receiver_portion, source_position, SOURCE_SPACING)  52.8 us
    all_to_all x1, waiting for transfers between devices, shards(): lax.all_to_all(adjoint_operator.reshape(1, freq_total, 2, receiver_portio...  48.6 us
    mul x1, other arithmetic, shards(): extended[:, offset:offset + source_position] * mask_block[None]  42 us
    all_to_all x1, waiting for transfers between devices, shards(): lax.all_to_all(regrouped_traces, ('node', 'freq'), split_axis=0, concat_a...  36.8 us
    add x1, other arithmetic, shards(): accumulated_total + jnp.pad(frame_block, ((0, 0), (offset, listen_segment...  23 us
    unnamed x44, local copies, waits for them, and re-layouts  18.6 us
  transfers between devices with their start and end apart: 4, of which 3 were waited for; matrix products, arithmetic and copies ran while one was open for 4% of the time, Pallas kernels for 0%

commit v1 on v0

v1 whole, which is shorter than its diff:
```python
import functools
import math

import jax
import jax.numpy as jnp
from jax import lax
from jax.experimental import pallas as pl
from jax.experimental.pallas import tpu as pltpu
from jax.sharding import PartitionSpec as P

LISTEN_SPAN = 4096
SOURCE_SPACING = 1024
LANES = 128
SPAN = LISTEN_SPAN // SOURCE_SPACING

relaxation = 0.25
ridge_scale = 0.001
highest = lax.Precision.HIGHEST


def inner_product(former, latter):
    return lax.dot_general(former, latter, (((1,), (1,)), ((), ())), precision=highest)


def outer_product(former, latter):
    return lax.dot_general(former, latter, (((0,), (0,)), ((), ())), precision=highest)


def reduce_rank(matrix, random_projector):
    real_part = matrix[0]
    imag_part = matrix[1]
    rank_count = random_projector.shape[1]
    proj_real = lax.dot_general(
        random_projector, real_part, (((0,), (1,)), ((), ())), precision=highest
    )
    proj_imag = lax.dot_general(
        random_projector, imag_part, (((0,), (1,)), ((), ())), precision=highest
    )
    gram_real = inner_product(proj_real, proj_real) + inner_product(proj_imag, proj_imag)
    gram_imag = inner_product(proj_real, proj_imag) - inner_product(proj_imag, proj_real)
    coef_real = jnp.dot(proj_real, real_part, precision=highest) + jnp.dot(
        proj_imag, imag_part, precision=highest
    )
    coef_imag = jnp.dot(proj_real, imag_part, precision=highest) - jnp.dot(
        proj_imag, real_part, precision=highest
    )
    system = jnp.concatenate(
        [jnp.concatenate([gram_real, -gram_imag], 1), jnp.concatenate([gram_imag, gram_real], 1)], 0
    )
    ridge_shift = ridge_scale * jnp.trace(gram_real) / rank_count
    system = system + ridge_shift * jnp.eye(2 * rank_count, dtype=system.dtype)
    right_side = jnp.concatenate([coef_real, coef_imag], 0)
    return system, right_side, proj_real, proj_imag


def restore(system, inverse, right_side, proj_real, proj_imag):
    rank_count = proj_real.shape[0]
    solved = jnp.dot(inverse, right_side, precision=highest)
    rest = right_side - jnp.dot(system, solved, precision=highest)
    solved = solved + jnp.dot(inverse, rest, precision=highest)
    solution_real = solved[:rank_count]
    solution_imag = solved[rank_count:]
    low_real = outer_product(proj_real, solution_real) - outer_product(proj_imag, solution_imag)
    low_imag = outer_product(proj_real, solution_imag) + outer_product(proj_imag, solution_real)
    return jnp.stack([low_real, low_imag])


def invert_kernel(system_ref, inverse_ref):
    count, size, _ = system_ref.shape
    held = [system_ref[m] for m in range(count)]
    lane = lax.broadcasted_iota(jnp.int32, (size, size), 1)
    line = lax.broadcasted_iota(jnp.int32, (size, size), 0)
    top = lax.broadcasted_iota(jnp.int32, (1, size), 1)
    for k in range(size):
        for m in range(count):
            a = held[m]
            pivot = 1.0 / a[k : k + 1, k : k + 1]
            row = jnp.where(top == k, pivot, a[k : k + 1, :] * pivot)
            rest = jnp.where(lane == k, 0.0, a) - a[:, k : k + 1] * row
            held[m] = jnp.where(line == k, row, rest)
    for m in range(count):
        inverse_ref[m] = held[m]


def pack_kernel(dims, src_ref, out_ref, flip):
    node_axis, freq_axis, nodes, shots, halo, per_row, rows, planes = dims
    parts = flip.shape[0]
    for part in range(parts):
        flip[part, :halo] = jnp.zeros((halo, LANES), jnp.float32)
    for plane in range(planes):
        for part in range(parts):
            flip[part, halo:] = src_ref[plane, part * LANES : (part + 1) * LANES].T
            for fb in range(freq_axis):
                picks = [
                    flip[part, pl.ds(fb * shots + i, rows, stride=per_row), :]
                    for i in range(per_row)
                ]
                for j in range(per_row):
                    nb = part * per_row + j
                    out_ref[nb * freq_axis + fb, plane * rows : (plane + 1) * rows, :] = (
                        jnp.concatenate([p[:, j * nodes : (j + 1) * nodes] for p in picks], 1)
                    )


def unpack_kernel(dims, packed_ref, src_ref, out_ref, flip):
    node_axis, freq_axis, nodes, shots, halo, per_row, rows, planes = dims
    parts = flip.shape[0]
    head = halo // per_row
    for plane in range(planes):
        for part in range(parts):
            for fb in range(freq_axis):
                pieces = [
                    packed_ref[
                        (part * per_row + j) * freq_axis + fb, plane * rows : (plane + 1) * rows, :
                    ]
                    for j in range(per_row)
                ]
                for i in range(per_row):
                    line = jnp.concatenate([p[:, i * nodes : (i + 1) * nodes] for p in pieces], 1)
                    start = fb * shots + i
                    if fb > 0:
                        at = pl.ds(start, head, stride=per_row)
                        flip[part, at, :] = flip[part, at, :] + line[:head]
                        flip[part, pl.ds(start + halo, rows - head, stride=per_row), :] = line[head:]
                    else:
                        flip[part, pl.ds(start, rows, stride=per_row), :] = line
            span = slice(part * LANES, (part + 1) * LANES)
            out_ref[plane, span] = src_ref[plane, span] + relaxation * flip[part, halo:].T


def swap_parts(x):
    even = lax.broadcasted_iota(jnp.int32, x.shape, 1) % 2 == 0
    width = x.shape[1]
    return jnp.where(even, pltpu.roll(x, width - 1, 1), pltpu.roll(x, 1, 1))


def split(x):
    hi = x.astype(jnp.bfloat16)
    return hi, (x - hi.astype(jnp.float32)).astype(jnp.bfloat16)


def split_table(x):
    hi = lax.reduce_precision(x, 8, 7)
    return hi.astype(jnp.bfloat16), (x - hi).astype(jnp.bfloat16)


def step_kernel(
    dims, per_step, dither, recv_ref, gather_ref, cos_ref, sin_ref, turn_ref, ahead_ref, back_ref,
    misfit_ref, packed_ref, coef, coef_swap, acc, frame,
):
    node_axis, freq_axis, nodes, shots, halo, per_row, rows, planes = dims
    bins = cos_ref.shape[1]
    step = pl.program_id(0)
    block = per_step * nodes

    @pl.when(step == 0)
    def _():
        acc[...] = jnp.zeros_like(acc)
        for r in range(rows):
            x = recv_ref[pl.ds(r, bins, stride=rows), :].T
            y = swap_parts(x)
            for i in range(per_row):
                l = r * per_row + i
                c = cos_ref[l : l + 1, :]
                s = sin_ref[l : l + 1, :]
                xi = x[i * nodes : (i + 1) * nodes]
                yi = y[i * nodes : (i + 1) * nodes]
                coef[l * nodes : (l + 1) * nodes] = xi * c + yi * s
                coef_swap[l * nodes : (l + 1) * nodes] = yi * c - xi * s

    base = step * per_step + halo
    def at(back):
        return pl.ds(pl.multiple_of((base - back) * nodes, nodes), block)

    steady = None
    for k in range(1, SPAN):
        a = turn_ref[k : k + 1, :]
        b = turn_ref[SPAN + k : SPAN + k + 1, :]
        term = coef[at(k), :] * a + coef_swap[at(k), :] * b
        steady = term if steady is None else steady + term
    hi, lo = split(jnp.concatenate([steady, coef[at(SPAN), :], coef[at(0), :]], 0))
    frame[...] = jnp.dot(
        jnp.concatenate([hi, lo, hi], 1), ahead_ref[...], preferred_element_type=jnp.float32
    )
    clock = lax.broadcasted_iota(jnp.int32, (1, SOURCE_SPACING), 1)
    full_hi, full_lo, old_hi, old_lo, new_hi, new_lo = [], [], [], [], [], []
    for i in range(per_step):
        leaving = clock < dither[base + i - SPAN]
        entering = clock >= dither[base + i]
        old_mask = leaving.astype(jnp.float32)
        new_mask = entering.astype(jnp.float32)
        row = slice(i * nodes, (i + 1) * nodes)
        mixed = (
            frame[i * nodes : (i + 1) * nodes]
            + frame[block + i * nodes : block + (i + 1) * nodes] * old_mask
            + frame[2 * block + i * nodes : 2 * block + (i + 1) * nodes] * new_mask
        )
        cols = slice(i * SOURCE_SPACING, (i + 1) * SOURCE_SPACING)
        misfit = gather_ref[:, cols] - mixed
        misfit_ref[:, cols] = misfit
        hi, lo = split(misfit)
        old_mask = old_mask.astype(jnp.bfloat16)
        new_mask = new_mask.astype(jnp.bfloat16)
        full_hi.append(hi)
        full_lo.append(lo)
        old_hi.append(hi * old_mask)
        old_lo.append(lo * old_mask)
        new_hi.append(hi * new_mask)
        new_lo.append(lo * new_mask)
    upper = jnp.concatenate(full_hi + old_hi + new_hi, 0)
    lower = jnp.concatenate(full_lo + old_lo + new_lo, 0)
    wide = jnp.dot(upper, back_ref[...], preferred_element_type=jnp.float32)
    narrow = jnp.dot(lower, back_ref[:, :bins], preferred_element_type=jnp.float32)
    total = wide[:, :bins] + wide[:, bins:] + narrow
    whole = total[:block]
    whole_swap = swap_parts(whole)
    for k in range(1, SPAN):
        a = turn_ref[k : k + 1, :]
        b = turn_ref[SPAN + k : SPAN + k + 1, :]
        acc[at(k), :] += whole * a - whole_swap * b
    acc[at(SPAN), :] += total[block : 2 * block]
    acc[at(0), :] += total[2 * block :]

    @pl.when(step == pl.num_programs(0) - 1)
    def _():
        for r in range(rows):
            x = acc[r * LANES : (r + 1) * LANES, :]
            y = swap_parts(x)
            parts = []
            for i in range(per_row):
                l = r * per_row + i
                c = cos_ref[l : l + 1, :]
                s = sin_ref[l : l + 1, :]
                parts.append(
                    x[i * nodes : (i + 1) * nodes] * c - y[i * nodes : (i + 1) * nodes] * s
                )
            packed_ref[pl.ds(r, bins, stride=rows), :] = jnp.concatenate(parts, 0).T


def shards(receiver_gathers, fourier_estimate, random_projector, release_sample):
    nodes, segment = receiver_gathers.shape
    freq_local, _, all_nodes, all_shots = fourier_estimate.shape
    shots = release_sample.shape[0]
    node_axis = lax.axis_size("node")
    freq_axis = lax.axis_size("freq")
    devices = node_axis * freq_axis
    planes = 2 * freq_local
    bins = planes * devices
    per_row = LANES // nodes
    rows = -(-(shots + SPAN) // per_row)
    while planes * rows % 8:
        rows += 1
    halo = rows * per_row - shots
    per_step = 8 if shots % 8 == 0 else 1
    dims = (node_axis, freq_axis, nodes, shots, halo, per_row, rows, planes)
    vmem = pltpu.VMEM
    whole = pl.BlockSpec(memory_space=vmem)
    params = pltpu.CompilerParams(vmem_limit_bytes=56 * 1024 * 1024)

    dither = release_sample % SOURCE_SPACING
    before = lax.ppermute(
        dither[shots - halo :], "freq", [(i, i + 1) for i in range(freq_axis - 1)]
    )
    dither = jnp.concatenate([before, dither])
    lane = lax.iota(jnp.int32, bins)
    column = lane // 2 + 1
    imag = lane % 2 == 1
    scale = 2.0 * math.pi / LISTEN_SPAN
    angle = scale * (dither[:, None] * column[None, :] % LISTEN_SPAN).astype(jnp.float32)
    cos_shift = jnp.cos(angle)
    sin_shift = jnp.where(imag[None, :], -jnp.sin(angle), jnp.sin(angle))
    quarter = column[None, :] * lax.iota(jnp.int32, SPAN)[:, None] % 4
    turn_same = jnp.where(quarter == 0, 1.0, jnp.where(quarter == 2, -1.0, 0.0))
    turn_cross = jnp.where(quarter == 1, -1.0, jnp.where(quarter == 3, 1.0, 0.0))
    turn_cross = jnp.where(imag[None, :], -turn_cross, turn_cross)
    turn = jnp.concatenate([turn_same, turn_cross], 0).astype(jnp.float32)
    clock = lax.iota(jnp.int32, SOURCE_SPACING)

    def table(phase, odd):
        theta = scale * (phase % LISTEN_SPAN).astype(jnp.float32)
        return jnp.where(odd, -jnp.sin(theta), jnp.cos(theta)) * (1.0 / math.sqrt(LISTEN_SPAN))

    ahead = table(column[:, None] * clock[None, :], imag[:, None])
    hi, lo = split_table(2.0 * ahead)
    ahead_table = jnp.concatenate([hi, hi, lo], 0)
    hi, lo = split_table(ahead.T)
    back_table = jnp.concatenate([hi, lo], 1)

    planar = fourier_estimate.reshape(planes, all_nodes, all_shots)
    packed = pl.pallas_call(
        functools.partial(pack_kernel, dims),
        out_shape=jax.ShapeDtypeStruct((devices, planes * rows, LANES), jnp.float32),
        in_specs=[whole],
        out_specs=whole,
        scratch_shapes=[vmem((all_nodes // LANES, halo + all_shots, LANES), jnp.float32)],
        compiler_params=params,
        name="pack",
    )(planar)
    arrived = lax.all_to_all(packed, ("node", "freq"), split_axis=0, concat_axis=0, tiled=True)
    width = per_step * SOURCE_SPACING
    misfit, spectra = pl.pallas_call(
        functools.partial(step_kernel, dims, per_step),
        grid=(shots // per_step,),
        out_shape=(
            jax.ShapeDtypeStruct((nodes, segment), jnp.float32),
            jax.ShapeDtypeStruct((bins * rows, LANES), jnp.float32),
        ),
        in_specs=[
            pl.BlockSpec(memory_space=pltpu.SMEM),
            whole,
            pl.BlockSpec((nodes, width), lambda i: (0, i)),
            whole,
            whole,
            whole,
            whole,
            whole,
        ],
        out_specs=(pl.BlockSpec((nodes, width), lambda i: (0, i)), whole),
        scratch_shapes=[
            vmem(((shots + halo) * nodes, bins), jnp.float32),
            vmem(((shots + halo) * nodes, bins), jnp.float32),
            vmem(((shots + halo) * nodes, bins), jnp.float32),
            vmem((3 * per_step * nodes, SOURCE_SPACING), jnp.float32),
        ],
        compiler_params=params,
        name="blend",
    )(
        dither, arrived.reshape(bins * rows, LANES), receiver_gathers, cos_shift, sin_shift, turn,
        ahead_table, back_table,
    )
    returned = lax.all_to_all(
        spectra.reshape(devices, planes * rows, LANES),
        ("node", "freq"),
        split_axis=0,
        concat_axis=0,
        tiled=True,
    )
    updated = pl.pallas_call(
        functools.partial(unpack_kernel, dims),
        out_shape=jax.ShapeDtypeStruct(planar.shape, jnp.float32),
        in_specs=[whole, whole],
        out_specs=whole,
        scratch_shapes=[vmem((all_nodes // LANES, halo + all_shots, LANES), jnp.float32)],
        compiler_params=params,
        name="unpack",
    )(returned, planar)
    updated = updated.reshape(fourier_estimate.shape)
    system, right_side, proj_real, proj_imag = jax.vmap(reduce_rank, in_axes=(0, None))(
        updated, random_projector
    )
    inverse = pl.pallas_call(
        invert_kernel,
        out_shape=jax.ShapeDtypeStruct(system.shape, jnp.float32),
        in_specs=[whole],
        out_specs=whole,
        compiler_params=params,
        name="invert",
    )(system)
    deblended = jax.vmap(restore)(system, inverse, right_side, proj_real, proj_imag)
    return (deblended, misfit)


def solution(mesh):
    return jax.shard_map(
        shards,
        mesh=mesh,
        in_specs=(P("node", "freq"), P(("node", "freq"), None, None, None), P(), P("freq")),
        out_specs=(P(("node", "freq"), None, None, None), P("node", "freq")),
        check_vma=False,
    )
```

time: 507 us -> 160 us (0.32); the launches traced: 497 us -> 160 us
  other arithmetic: 180 us -> 9.16 us
  matrix products: 147 us -> 13.7 us
  local copies, waits for them, and re-layouts: 58.6 us -> 3.73 us
  Pallas kernels: 0 us -> 49.2 us
  waiting for transfers between devices: 89.2 us -> 69.9 us
  starting transfers between devices: 20.8 us -> 13.4 us
    dot_general x10 -> x3, matrix products: 138 us -> 3.05 us  [the longest x1 1.36 us: restore(): solved = jnp.dot(inverse, right_side, precision=highest)]
    mul x6 -> x0, other arithmetic: 100 us -> none  [the longest x3 52.8 us: shards(): frame_block.reshape(receiver_portion, source_position, SOURCE_SPACING)]
    pallas_call x0 -> x4, Pallas kernels: none -> 49.2 us  [the longest x1 29.5 us: shards(): pl.pallas_call(functools.partial(step_kernel, dims, per_step), grid=(shot...]
    another operation x9 -> x0, other arithmetic: 34.6 us -> none  [the longest x4 17.8 us: reduce_rank(): factor = jnp.linalg.cholesky(system)]
    add x6 -> x1, other arithmetic: 28.1 us -> 0.01 us  [shards(): column = lane // 2 + 1]
    reshape x5 -> x0, local copies, waits for them, and re-layouts: 20.5 us -> none  [the longest x1 10.4 us: shards(): jnp.concatenate([misfit_signal, heads], 1)]
    all_to_all x2, waiting for transfers between devices: 85.4 us -> 69.9 us  [the longest x1 40.1 us: shards(): lax.all_to_all(spectra.reshape(devices, planes * rows, LANES), ('node', '...]
    unnamed x44 -> x15, local copies, waits for them, and re-layouts: 18.6 us -> 3.66 us
  transfers between devices with their start and end apart: 4 -> 3, of which waited for: 3 -> 2; matrix products, arithmetic and copies ran while one was open for 4% -> 5% of each run, Pallas kernels for 0% -> 0%
where the time goes in v1:
time: 160 us
  waiting for transfers between devices  69.9 us (44%)
  Pallas kernels  49.2 us (31%)
  matrix products  13.7 us (9%)
  starting transfers between devices  13.4 us (8%)
  other arithmetic  9.16 us (6%)
  local copies, waits for them, and re-layouts  3.73 us (2%)
    all_to_all x1, waiting for transfers between devices, shards(): lax.all_to_all(spectra.reshape(devices, planes * rows, LANES), ('node', '...  40.1 us
    all_to_all x1, waiting for transfers between devices, shards(): lax.all_to_all(packed, ('node', 'freq'), split_axis=0, concat_axis=0, til...  29.8 us
    pallas_call x1, Pallas kernels, shards(): pl.pallas_call(functools.partial(step_kernel, dims, per_step), grid=(shot...  29.5 us
    pallas_call x1, Pallas kernels, shards(): pl.pallas_call(invert_kernel, out_shape=jax.ShapeDtypeStruct(system.shape...  9.72 us
    all_to_all x1, starting transfers between devices, shards(): lax.all_to_all(packed, ('node', 'freq'), split_axis=0, concat_axis=0, til...  7.3 us
    pallas_call x1, Pallas kernels, shards(): pl.pallas_call(functools.partial(unpack_kernel, dims), out_shape=jax.Shap...  5.3 us
    convert_element_type x2, other arithmetic, split_table(): return (hi.astype(jnp.bfloat16), (x - hi).astype(jnp.bfloat16))  4.78 us
    pallas_call x1, Pallas kernels, shards(): pl.pallas_call(functools.partial(pack_kernel, dims), out_shape=jax.ShapeD...  4.74 us
  transfers between devices with their start and end apart: 3, of which 2 were waited for; matrix products, arithmetic and copies ran while one was open for 5% of the time, Pallas kernels for 0%

profile of v1, /device:TPU:0, one launch (start us, length us, event | category | flops | bytes accessed | tf_op | source)
XLA Modules:
  0.0 159.9 jit_solution(4740396619271519545)
XLA Ops:
  0.6 4.7 %pack.1 = f32[32,104,128]{2,1,0:T(8,128)} custom-call(f32[4,256,384]{2,1,0:T(8,128)} %bitcast.73), custom_call_target="tpu_custom_call" | custom-call | tf_op jit(solution)/shard_map/pack/pallas_call | solution.py:290
  5.4 7.3 %all-to-all-start = ((f32[32,104,128]{2,1,0:T(8,128)}), f32[32,104,128]{2,1,0:T(8,128)S(1)}, u32[]{:S(2)}, u32[]{:S(2)}) async-start(f32[32,104,128]{2,1,0:T(8,128)} %pack.1), calls=%async_computation | async-start | bytes 3407872 | tf_op jit(solution)/shard_map/all_to_all | solution.py:299
  12.8 2.1 %collective-permute-start = (s32[8]{0:T(128)S(1)}, s32[8]{0:T(128)S(1)}, u32[]{:S(2)}, u32[]{:S(2)}) collective-permute-start(s32[8]{0:T(128)S(1)} %slice.15), channel_id=1, source_target_pairs={{0,1},{1,2},{2,3},{4,5},{5,6},{6,7},{8,9},{9,10},{10,11},{12,13},{... | collective-permute-start | bytes 104 | tf_op jit(solution)/shard_map/ppermute | solution.py:261
  15.0 0.6 pad_maximum_fusion.4.turn_ref
  15.6 2.3 %reduce-precision_convert_fusion = (bf16[1024,128]{1,0:T(8,128)(2,1)S(1)}, bf16[1024,128]{1,0:T(8,128)(2,1)S(1)}) fusion(s32[128]{0:T(128)S(1)} %fusion.48, pred[128]{0:T(512)(128)(4,1)S(1)} %fusion.47), kind=kLoop, calls=%fused_computation.21 | loop fusion | flops 2752512 | bytes 524928 | tf_op jit(solution)/shard_map/convert_element_type | solution.py:144
  17.9 0.9 pad_maximum_fusion.1.back_ref
  18.7 2.5 %reduce-precision_convert_fusion.1 = (bf16[128,1024]{1,0:T(8,128)(2,1)S(1)}, bf16[128,1024]{1,0:T(8,128)(2,1)S(1)}) fusion(s32[128]{0:T(128)S(1)} %fusion.48, pred[128]{0:T(512)(128)(4,1)S(1)} %fusion.47), kind=kLoop, calls=%fused_computation.23 | loop fusion | flops 2752512 | bytes 524928 | tf_op jit(solution)/shard_map/convert_element_type | solution.py:144
  21.2 1.0 pad_maximum_fusion.ahead_ref
  22.3 1.0 negate_select_fusion.4
  23.3 29.8 %all-to-all-done = f32[32,104,128]{2,1,0:T(8,128)S(1)} async-done(((f32[32,104,128]{2,1,0:T(8,128)}), f32[32,104,128]{2,1,0:T(8,128)S(1)}, u32[]{:S(2)}, u32[]{:S(2)}) %all-to-all-start) | async-done | bytes 1703968 | tf_op jit(solution)/shard_map/all_to_all | solution.py:299
  53.0 1.2 copy-done.2
  54.2 29.5 %blend.1 = (f32[32,98304]{1,0:T(8,128)}, f32[3328,128]{1,0:T(8,128)}) custom-call(s32[104]{0:T(128)} %copy-done.5, f32[3328,128]{1,0:T(8,128)} %bitcast.72, f32[32,98304]{1,0:T(8,128)} %gather_ref.1, f32[104,128]{1,0:T(8,128)} %get-tuple-element.13.cos_ref, f32[104,128]{1,0:T(8,128)} %get-tuple-element.12.sin_ref, f32[8,128]{1,0:T(8,128)} %pad_maximum_fusion.4.turn_ref, ...), custom_call_target="tpu_custom_call" | custom-call | tf_op jit(solution)/shard_map/blend/pallas_call | solution.py:301
  83.7 4.0 %all-to-all-start.1 = ((f32[32,104,128]{2,1,0:T(8,128)}), f32[32,104,128]{2,1,0:T(8,128)S(1)}, u32[]{:S(2)}, u32[]{:S(2)}) async-start(f32[32,104,128]{2,1,0:T(8,128)} %bitcast.75), calls=%async_computation.1 | async-start | bytes 3407872 | tf_op jit(solution)/shard_map/all_to_all | solution.py:331
  87.7 40.1 %all-to-all-done.1.packed_ref = f32[32,104,128]{2,1,0:T(8,128)S(1)} async-done(((f32[32,104,128]{2,1,0:T(8,128)}), f32[32,104,128]{2,1,0:T(8,128)S(1)}, u32[]{:S(2)}, u32[]{:S(2)}) %all-to-all-start.1) | async-done | bytes 1703968 | tf_op jit(solution)/shard_map/all_to_all | solution.py:331
  127.8 1.2 copy-done.3
  129.0 5.3 %unpack.1 = f32[4,256,384]{2,1,0:T(8,128)} custom-call(f32[32,104,128]{2,1,0:T(8,128)} %copy-done.3, f32[4,256,384]{2,1,0:T(8,128)} %bitcast.74), custom_call_target="tpu_custom_call" | custom-call | tf_op jit(solution)/shard_map/unpack/pallas_call | solution.py:338
  134.3 2.1 %fusion.3 = f32[2,256,48]{1,2,0:T(8,128)S(1)} fusion(f32[2,2,256,384]{3,2,1,0:T(8,128)} %bitcast.66, f32[384,48]{0,1:T(8,128)S(1)} %copy-done), kind=kOutput, calls=%fused_computation.25 | convolution fusion | flops 113246208 | bytes 958464 | tf_op jit(solution)/shard_map/vmap()/dot_general | solution.py:33
  136.4 2.0 %fusion.5 = f32[2,256,48]{1,2,0:T(8,128)S(1)} fusion(f32[2,2,256,384]{3,2,1,0:T(8,128)} %bitcast.67, f32[384,48]{0,1:T(8,128)S(1)} %copy-done), kind=kOutput, calls=%fused_computation.27 | convolution fusion | flops 113246208 | bytes 958464 | tf_op jit(solution)/shard_map/vmap()/dot_general | solution.py:36
  138.5 0.5 fusion.2
  139.0 0.5 fusion.4
  140.0 0.5 convolution_add_fusion.2
  140.5 0.5 convolution_subtract_fusion.2
  141.6 0.7 maximum_add_fusion.system_ref
  142.4 9.7 %invert.1 = f32[2,96,96]{2,1,0:T(8,128)} custom-call(f32[2,96,96]{2,1,0:T(8,128)} %maximum_add_fusion.system_ref), custom_call_target="tpu_custom_call" | custom-call | tf_op jit(solution)/shard_map/invert/pallas_call | solution.py:351
  152.1 1.4 fusion.20
  153.5 1.3 convolution_subtract_fusion.1
  154.8 0.4 convolution_add_fusion.1
  155.2 0.8 fusion.25
  156.0 0.8 fusion.21
  156.9 0.8 fusion.1
  157.7 0.8 fusion
  158.7 1.2 copy.8
  (27 shorter events, 1.4 us)
Async XLA Ops:
  0.6 133.7 %copy-start = (f32[384,48]{0,1:T(8,128)S(1)}, f32[384,48]{0,1:T(8,128)}, u32[]{:S(2)}) copy-start(f32[384,48]{0,1:T(8,128)} %param.6) | copy-start | bytes 221188
  5.4 7.3 %copy-start.6 = (s32[96]{0:T(128)S(1)}, s32[96]{0:T(128)}, u32[]{:S(2)}) copy-start(s32[96]{0:T(128)} %param.7) | copy-start | bytes 1156
  5.4 47.6 %all-to-all-start = ((f32[32,104,128]{2,1,0:T(8,128)}), f32[32,104,128]{2,1,0:T(8,128)S(1)}, u32[]{:S(2)}, u32[]{:S(2)}) async-start(f32[32,104,128]{2,1,0:T(8,128)} %pack.1), calls=%async_computation | async-start | bytes 3407872 | tf_op jit(solution)/shard_map/all_to_all | solution.py:299
  12.8 9.4 %collective-permute-start = (s32[8]{0:T(128)S(1)}, s32[8]{0:T(128)S(1)}, u32[]{:S(2)}, u32[]{:S(2)}) collective-permute-start(s32[8]{0:T(128)S(1)} %slice.15), channel_id=1, source_target_pairs={{0,1},{1,2},{2,3},{4,5},{5,6},{6,7},{8,9},{9,10},{10,11},{12,13},{... | collective-permute-start | bytes 104 | tf_op jit(solution)/shard_map/ppermute | solution.py:261
  22.3 30.7 %copy-start.5 = (s32[104]{0:T(128)}, s32[104]{0:T(128)S(1)}, u32[]{:S(2)}) copy-start(s32[104]{0:T(128)S(1)} %pad_add_fusion.dither) | copy-start | bytes 1252
  53.0 1.2 copy-start.2
  83.7 44.1 %all-to-all-start.1 = ((f32[32,104,128]{2,1,0:T(8,128)}), f32[32,104,128]{2,1,0:T(8,128)S(1)}, u32[]{:S(2)}, u32[]{:S(2)}) async-start(f32[32,104,128]{2,1,0:T(8,128)} %bitcast.75), calls=%async_computation.1 | async-start | bytes 3407872 | tf_op jit(solution)/shard_map/all_to_all | solution.py:331
  127.8 1.2 copy-start.3
  134.3 4.2 %copy-start.1 = (f32[4,256,384]{2,1,0:T(8,128)S(1)}, f32[4,256,384]{2,1,0:T(8,128)}, u32[]{:S(2)}) copy-start(f32[4,256,384]{2,1,0:T(8,128)} %unpack.1) | copy-start | bytes 4718596
  152.1 2.7 %copy-start.4 = (f32[2,96,96]{2,1,0:T(8,128)S(1)}, f32[2,96,96]{2,1,0:T(8,128)}, u32[]{:S(2)}) copy-start(f32[2,96,96]{2,1,0:T(8,128)} %invert.1) | copy-start | bytes 221188
